TPU v7x, 32 devices: a whole 2x2x4 slice. The times are simulated.
32 devices in a mesh: replica: 4 (over z), fsdp: 8 (over y, x, core).
Axes of the slice: x: 2, y: 2, z: 4, core: 2. Of those that a mesh axis runs over, the one named last changes fastest.
Arguments:
- grads: bfloat16 [4, 20, 704, 1024], P('replica', None, 'fsdp'), may hold values from -20 to 20
- momentum: bfloat16 [20, 704, 1024], P('replica', 'fsdp'), may hold values from -3 to 3
- weight: bfloat16 [20, 704, 1024], P('replica', 'fsdp'), may hold values from -6 to 6
- owners: int32 [20], replicated, may hold values from 0 to 8, as said below
Outputs:
- new_momentum: bfloat16 [20, 704, 1024], P('replica', 'fsdp')
- update: bfloat16 [20, 704, 1024], P('replica', 'fsdp')
- new_weight: bfloat16 [20, 704, 1024], P('replica', 'fsdp')
Inputs may be any that keep to these rules, and one draw needn't show every extreme that they name: `owners`: matrices 5 * r to 5 * (r + 1) - 1 form group r. Within a group no value below 8 is named by more than 2 matrices, and some value by exactly 2.
All inputs are finite; a program needn't handle non-finite values.
Results may differ from a plain program's by a relative error of at most 0.018.
Values may be sent and summed in bfloat16 or wider, within the bound.
A program may use at most 64 MiB of HBM per device.

v0:
```python
import math

import jax
import jax.numpy as jnp
from jax import lax
from jax.sharding import PartitionSpec as P

ITERS = 2
CAP = 2


EPSILON = 1e-07
COEFF_LINEAR = 3.4445
COEFF_CUBIC = -4.775
COEFF_QUINTIC = 2.0315
MOMENTUM_DECAY = 0.95
LEARN_RATE = 0.02
DECAY_RATE = 0.1
UPDATE_RATIO = 0.2


def newton_blocks(blocks):
    scaled = blocks.astype(jnp.float32)
    frobenius = jnp.sqrt(jnp.sum(scaled * scaled, axis=(1, 2), keepdims=True))
    iterate = lax.optimization_barrier((scaled / (frobenius + EPSILON)).astype(jnp.bfloat16))
    for turn in range(ITERS):
        gram_matrix = jnp.einsum(
            "cik,cjk->cij", iterate, iterate, preferred_element_type=jnp.float32
        ).astype(jnp.bfloat16)
        gram_matrix = lax.optimization_barrier(gram_matrix)
        gram_square = jnp.einsum(
            "cij,cjk->cik", gram_matrix, gram_matrix, preferred_element_type=jnp.float32
        )
        poly_term = (
            COEFF_CUBIC * gram_matrix.astype(jnp.float32) + COEFF_QUINTIC * gram_square
        ).astype(jnp.bfloat16)
        product = jnp.einsum("cij,cjk->cik", poly_term, iterate, preferred_element_type=jnp.float32)
        iterate = (COEFF_LINEAR * iterate.astype(jnp.float32) + product).astype(jnp.bfloat16)
        iterate = lax.optimization_barrier(iterate)
    return iterate


def newton_items(received):
    return newton_blocks(received[0])[None]


def on_device(grads, momentum, weight, owners):
    groups = lax.axis_size("fsdp")
    summed = lax.psum_scatter(
        grads[0].astype(jnp.float32).astype(jnp.bfloat16),
        "replica",
        scatter_dimension=0,
        tiled=True,
    ).astype(jnp.float32)
    local_count = momentum.shape[0]
    row_count = momentum.shape[1]
    col_count = momentum.shape[2]
    offset = lax.axis_index("replica") * local_count
    group_owners = lax.dynamic_slice_in_dim(owners, offset, local_count)
    active = group_owners < groups
    keep_mask = active[:, None, None]
    old_momentum = momentum.astype(jnp.float32)
    new_momentum = jnp.where(
        keep_mask, MOMENTUM_DECAY * old_momentum + summed, old_momentum
    ).astype(jnp.bfloat16)
    stored = lax.optimization_barrier(new_momentum)
    outgoing = (summed + MOMENTUM_DECAY * stored.astype(jnp.float32)).astype(jnp.bfloat16)
    position = jnp.arange(local_count)
    earlier = (group_owners[:, None] == group_owners[None, :]) & (
        position[None, :] < position[:, None]
    )
    slot_index = jnp.sum(earlier.astype(jnp.int32), axis=1)
    capacity = CAP
    slot_code = jnp.where(active, group_owners * capacity + slot_index, -1)
    one_hot = (slot_code[None, :] == jnp.arange(groups * capacity)[:, None]).astype(jnp.bfloat16)
    flattened = outgoing.reshape(local_count, row_count * col_count)
    packed = jnp.dot(one_hot, flattened, preferred_element_type=jnp.float32).astype(jnp.bfloat16)
    packed = packed.reshape(groups, capacity, row_count, col_count)
    orthogonal = newton_items(
        lax.all_to_all(packed, "fsdp", split_axis=0, concat_axis=2, tiled=True)
    )
    returned = lax.all_to_all(orthogonal, "fsdp", split_axis=2, concat_axis=0, tiled=True)
    restored = jnp.dot(
        one_hot.T,
        returned.reshape(groups * capacity, row_count * col_count),
        preferred_element_type=jnp.float32,
    )
    restored = restored.reshape(local_count, row_count, col_count)
    update_scale = UPDATE_RATIO * math.sqrt(max(row_count * groups, col_count))
    update = (update_scale * restored).astype(jnp.bfloat16)
    old_weight = weight.astype(jnp.float32)
    stepped = old_weight * (1.0 - LEARN_RATE * DECAY_RATE) - LEARN_RATE * update_scale * restored
    new_weight = jnp.where(keep_mask, stepped, old_weight).astype(jnp.bfloat16)
    return (new_momentum, update, new_weight)


def solution(mesh):
    in_specs = (
        P("replica", None, "fsdp", None),
        P("replica", "fsdp", None),
        P("replica", "fsdp", None),
        P(),
    )
    out_specs = (P("replica", "fsdp", None), P("replica", "fsdp", None), P("replica", "fsdp", None))
    return jax.shard_map(
        on_device, mesh=mesh, in_specs=in_specs, out_specs=out_specs, check_vma=False
    )
```

profile of v0, /device:TPU:1, one launch (start us, length us, event | category | flops | bytes accessed | tf_op | source)
XLA Modules:
  0.0 219.4 jit_solution(8990422567662260606)
XLA Ops:
  7.2 0.0 copy-start.3
  7.2 0.0 copy-start.2
  7.2 0.0 reduce-scatter.2.cloned.1.call-start
  7.2 0.7 reduce-scatter.2.cloned.1.call-update
  7.9 0.0 copy-done.3
  7.9 0.1 broadcast_compare_fusion
  8.0 0.2 convert_reduce_fusion
  8.2 71.5 %reduce-scatter.2.cloned.1.call-done = bf16[5,88,1024]{2,1,0:T(8,128)(2,1)} async-done(((bf16[20,88,1024]{2,1,0:T(8,128)(2,1)}), bf16[5,88,1024]{2,1,0:T(8,128)(2,1)}) %reduce-scatter.2.cloned.1.call-update) | async-done | bytes 901136 | tf_op jit(solution)/shard_map/reduce_scatter | solution.py:49
  79.7 0.0 copy-done.2
  79.7 2.5 %fusion.1 = bf16[5,88,1024]{2,0,1:T(8,128)(2,1)S(1)} fusion(bf16[5,88,1024]{2,1,0:T(8,128)(2,1)} %reduce-scatter.2.cloned.1.call-done, bf16[5,88,1024]{2,1,0:T(8,128)(2,1)S(1)} %copy-done.2, pred[5]{0:T(512)(128)(4,1)S(1)} %get-tuple-element.15), kind=kLoop, calls=%fused_computation.15 | loop fusion | flops 2703360 | bytes 2703365 | tf_op jit(solution)/shard_map/convert_element_type | solution.py:65
  82.2 1.0 fusion.2
  83.1 1.4 convolution_convert_fusion
  84.5 1.6 copy.44
  86.1 38.0 %all_to_all.24 = bf16[8,2,88,1024]{3,2,1,0:T(8,128)(2,1)S(1)} all-to-all(bf16[8,2,88,1024]{3,2,1,0:T(8,128)(2,1)S(1)} %bitcast.46), channel_id=1, replica_groups=mesh['replica'=4,'fsdp'=8] {'fsdp'}, dimensions={0} | all-to-all | bytes 5767168 | tf_op jit(solution)/shard_map/all_to_all | solution.py:80
  124.1 0.9 fusion
  125.0 0.7 convert_bitcast_fusion
  125.7 1.0 copy.35
  126.7 0.9 divide_convert_fusion
  127.7 0.0 copy-start.1
  127.7 1.6 copy-done.1
  129.3 3.8 %convolution_convert_fusion.2 = bf16[2,704,704]{2,1,0:T(8,128)(2,1)} fusion(bf16[2,704,1024]{2,1,0:T(8,128)(2,1)S(1)} %divide_convert_fusion), kind=kOutput, calls=%fused_computation.24 | convolution fusion | flops 2031034368 | bytes 4866048 | tf_op jit(solution)/shard_map/cik,cjk->cij/dot_general | solution.py:27
  133.1 10.4 %add_convert_fusion.1 = bf16[2,704,1024]{2,1,0:T(8,128)(2,1)} fusion(bf16[2,704,1024]{2,1,0:T(8,128)(2,1)} %copy-done.1, bf16[2,704,704]{2,1,0:T(8,128)(2,1)} %convolution_convert_fusion.2), kind=kOutput, calls=%fused_computation.5 | convolution fusion | flops 3436421120 | bytes 7749632 | tf_op jit(solution)/shard_map/cij,cjk->cik/dot_general | solution.py:37
  143.5 6.4 %convolution_convert_fusion.1 = bf16[2,704,704]{2,1,0:T(8,128)(2,1)} fusion(bf16[2,704,1024]{2,1,0:T(8,128)(2,1)} %add_convert_fusion.1), kind=kOutput, calls=%fused_computation.23 | convolution fusion | flops 2031034368 | bytes 4866048 | tf_op jit(solution)/shard_map/cik,cjk->cij/dot_general | solution.py:27
  149.9 10.7 %add_convert_fusion = bf16[2,704,1024]{2,1,0:T(8,128)(2,1)} fusion(bf16[2,704,1024]{2,1,0:T(8,128)(2,1)} %add_convert_fusion.1, bf16[2,704,704]{2,1,0:T(8,128)(2,1)} %convolution_convert_fusion.1), kind=kOutput, calls=%fused_computation.4 | convolution fusion | flops 3436421120 | bytes 7749632 | tf_op jit(solution)/shard_map/cij,cjk->cik/dot_general | solution.py:37
  160.6 6.4 %copy.36 = bf16[1,2,704,1024]{3,1,0,2:T(2,128)(2,1)} copy(bf16[1,2,704,1024]{3,2,1,0:T(8,128)(2,1)} %bitcast.50) | data formatting | bytes 5767168 | tf_op jit(solution)/shard_map/broadcast_in_dim | solution.py:44
  167.0 5.6 %all-to-all-start.1 = ((bf16[1,2,704,1024]{3,1,0,2:T(2,128)(2,1)}), bf16[1,2,704,1024]{3,1,0,2:T(2,128)(2,1)}, u32[]{:S(2)}, u32[]{:S(2)}) async-start(bf16[1,2,704,1024]{3,1,0,2:T(2,128)(2,1)} %copy.36), calls=%async_computation.2 | async-start | bytes 5767168 | tf_op jit(solution)/shard_map/all_to_all | solution.py:82
  172.6 1.5 copy.40
  174.1 30.1 %all-to-all-done.1 = bf16[1,2,704,1024]{3,1,0,2:T(2,128)(2,1)} async-done(((bf16[1,2,704,1024]{3,1,0,2:T(2,128)(2,1)}), bf16[1,2,704,1024]{3,1,0,2:T(2,128)(2,1)}, u32[]{:S(2)}, u32[]{:S(2)}) %all-to-all-start.1) | async-done | bytes 2883616 | tf_op jit(solution)/shard_map/all_to_all | solution.py:82
  204.2 2.8 %copy.37 = bf16[1,2,8,88,1024]{4,3,1,2,0:T(8,128)(2,1)S(1)} copy(bf16[1,2,8,88,1024]{4,1,3,2,0:T(2,128)(2,1)} %bitcast.7) | data formatting | bytes 5767168 | tf_op jit(solution)/shard_map/all_to_all | solution.py:82
  207.0 2.6 %fusion.4 = (bf16[5,88,1024]{2,0,1:T(8,128)(2,1)S(1)}, bf16[5,88,1024]{2,0,1:T(8,128)(2,1)S(1)}) fusion(bf16[5,88,1024]{2,1,0:T(8,128)(2,1)S(1)} %copy-done.4, pred[5]{0:T(512)(128)(4,1)S(1)} %get-tuple-element.15, s32[5]{0:T(128)S(1)} %add_select_fusion, bf16[2,8,88,1024]{3,2,1,0:T(8,128)(2,1)S(1)} %bitcast.49), kind=kOutput, calls=%fused_computation.18 | convolution fusion | flops 18022480 | bytes 5586969 | tf_op jit(solution)/shard_map/dot_general | solution.py:83
  209.5 1.5 copy.42
  211.1 1.5 copy.41
  (6 shorter events, 0.0 us)
Async XLA Ops:
  7.2 0.8 copy-start.3
  7.2 72.5 %copy-start.2 = (bf16[5,88,1024]{2,1,0:T(8,128)(2,1)S(1)}, bf16[5,88,1024]{2,1,0:T(8,128)(2,1)}, u32[]{:S(2)}) copy-start(bf16[5,88,1024]{2,1,0:T(8,128)(2,1)} %param.5) | copy-start | bytes 2703364
  7.2 72.5 %reduce-scatter.2.cloned.1.call-start = ((), (), s32[]{:S(2)}) async-start(), calls=%async_computation.3 | async-start | bytes 4505600 | tf_op jit(solution)/shard_map/reduce_scatter | solution.py:49
  79.7 2.5 %copy-start = (bf16[5,88,1024]{2,1,0:T(8,128)(2,1)S(1)}, bf16[5,88,1024]{2,1,0:T(8,128)(2,1)}, u32[]{:S(2)}) copy-start(bf16[5,88,1024]{2,1,0:T(8,128)(2,1)} %reduce-scatter.2.cloned.1.call-done) | copy-start | bytes 2703364
  127.7 1.6 copy-start.1
  167.0 37.2 %all-to-all-start.1 = ((bf16[1,2,704,1024]{3,1,0,2:T(2,128)(2,1)}), bf16[1,2,704,1024]{3,1,0,2:T(2,128)(2,1)}, u32[]{:S(2)}, u32[]{:S(2)}) async-start(bf16[1,2,704,1024]{3,1,0,2:T(2,128)(2,1)} %copy.36), calls=%async_computation.2 | async-start | bytes 5767168 | tf_op jit(solution)/shard_map/all_to_all | solution.py:82
  204.2 2.8 %copy-start.4 = (bf16[5,88,1024]{2,1,0:T(8,128)(2,1)S(1)}, bf16[5,88,1024]{2,1,0:T(8,128)(2,1)}, u32[]{:S(2)}) copy-start(bf16[5,88,1024]{2,1,0:T(8,128)(2,1)} %param.6) | copy-start | bytes 2703364
Sparse Core Ops, SparseCore 0:
  10.3 69.2 reduce-scatter.1
where the time goes:
time: 223 us; the launch traced here: 219 us
  waiting for transfers between devices  102 us (46%)
  blocking collectives  38 us (17%)
  matrix products  35.3 us (16%)
  local copies, waits for them, and re-layouts  17.9 us (8%)
  between operations  14.1 us (6%)
  other arithmetic  6.23 us (3%)
  starting transfers between devices  5.68 us (3%)
    reduce_scatter x1, waiting for transfers between devices, on_device(): lax.psum_scatter(grads[0].astype(jnp.float32).astype(jnp.bfloat16), 'repl...  71.5 us
    all_to_all x1, blocking collectives, on_device(): lax.all_to_all(packed, 'fsdp', split_axis=0, concat_axis=2, tiled=True)  38 us
    all_to_all x1, waiting for transfers between devices, on_device(): lax.all_to_all(orthogonal, 'fsdp', split_axis=2, concat_axis=0, tiled=True)  30.1 us
    dot_general x2, matrix products, newton_blocks(): jnp.einsum('cij,cjk->cik', poly_term, iterate, preferred_element_type=jnp...  21.1 us
    dot_general x2, matrix products, newton_blocks(): jnp.einsum('cik,cjk->cij', iterate, iterate, preferred_element_type=jnp.f...  10.2 us
    unnamed x14, local copies, waits for them, and re-layouts  7.75 us
    broadcast_in_dim x1, local copies, waits for them, and re-layouts, newton_items(): return newton_blocks(received[0])[None]  6.35 us
    all_to_all x1, starting transfers between devices, on_device(): lax.all_to_all(orthogonal, 'fsdp', split_axis=2, concat_axis=0, tiled=True)  5.64 us
  transfers between devices with their start and end apart: 2, of which 2 were waited for; matrix products, arithmetic and copies ran while one was open for 1% of the time, Pallas kernels for 0%

commit v1 on v0

v1 whole, which is shorter than its diff:
```python
import functools
import math

import jax
import jax.numpy as jnp
from jax import lax
from jax.experimental import pallas as pl
from jax.experimental.pallas import tpu as pltpu
from jax.sharding import PartitionSpec as P

ITERS = 2
ROW_TILE = 8
KERNEL_VMEM = 56 * 1024 * 1024


EPSILON = 1e-07
COEFF_LINEAR = 3.4445
COEFF_CUBIC = -4.775
COEFF_QUINTIC = 2.0315
MOMENTUM_DECAY = 0.95
LEARN_RATE = 0.02
DECAY_RATE = 0.1
UPDATE_RATIO = 0.2


def newton_blocks(blocks):
    scaled = blocks.astype(jnp.float32)
    frobenius = jnp.sqrt(jnp.sum(scaled * scaled, axis=(1, 2), keepdims=True))
    iterate = lax.optimization_barrier((scaled / (frobenius + EPSILON)).astype(jnp.bfloat16))
    for turn in range(ITERS):
        gram_matrix = jnp.einsum(
            "cik,cjk->cij", iterate, iterate, preferred_element_type=jnp.float32
        ).astype(jnp.bfloat16)
        gram_matrix = lax.optimization_barrier(gram_matrix)
        gram_square = jnp.einsum(
            "cij,cjk->cik", gram_matrix, gram_matrix, preferred_element_type=jnp.float32
        )
        poly_term = (
            COEFF_CUBIC * gram_matrix.astype(jnp.float32) + COEFF_QUINTIC * gram_square
        ).astype(jnp.bfloat16)
        product = jnp.einsum("cij,cjk->cik", poly_term, iterate, preferred_element_type=jnp.float32)
        iterate = (COEFF_LINEAR * iterate.astype(jnp.float32) + product).astype(jnp.bfloat16)
        iterate = lax.optimization_barrier(iterate)
    return iterate


def add_rows(left, right):
    return left.astype(jnp.float32) + right.astype(jnp.float32)


def fused_kernel(
    n_rep,
    n_fsdp,
    count,
    coef_ref,
    grads_ref,
    momentum_ref,
    stored_out,
    orth_out,
    own,
    old,
    from_left,
    from_right,
    total,
    stored,
    outgoing,
    gathered,
    iterate,
    gram,
    poly,
    finished,
    returned,
    load_sem,
    right_send,
    right_recv,
    left_send,
    left_recv,
    gather_send,
    gather_recv,
    return_send,
    return_recv,
    out_sem,
):
    rep = lax.axis_index("replica")
    me = lax.axis_index("fsdp")
    row_count, col_count = own.shape[1:]
    chips = n_fsdp // 2

    def owner_of(mat):
        return lax.rem(mat, chips) * 2 + mat // chips

    mine = lax.rem(me, 2) * chips + me // 2
    is_owner = mine < count
    turn_of_mine = jnp.where(
        mine < count - 3, mine + 1, jnp.where(mine < count - 1, count - 1, count)
    )

    load_grads = pltpu.make_async_copy(grads_ref, own, load_sem.at[0])
    load_old = pltpu.make_async_copy(momentum_ref, old, load_sem.at[1])
    load_grads.start()
    load_old.start()

    barrier = pltpu.get_barrier_semaphore()
    for step in range(1, n_fsdp):
        pl.semaphore_signal(barrier, inc=1, device_id={"fsdp": lax.rem(me + step, n_fsdp)})

    @pl.when(rep > 0)
    def _():
        pl.semaphore_signal(barrier, inc=1, device_id={"replica": rep - 1})

    @pl.when(rep < n_rep - 1)
    def _():
        pl.semaphore_signal(barrier, inc=1, device_id={"replica": rep + 1})

    inner = (rep > 0) & (rep < n_rep - 1)
    pl.semaphore_wait(barrier, jnp.where(inner, n_fsdp + 1, n_fsdp))

    load_grads.wait()
    load_old.wait()

    def right_copy(group, mat, raw=False):
        return pltpu.make_async_remote_copy(
            src_ref=own.at[group * count + mat] if raw else from_left.at[group, mat],
            dst_ref=from_left.at[group, mat],
            send_sem=right_send.at[group, mat],
            recv_sem=right_recv.at[group, mat],
            device_id={"replica": rep + 1},
        )

    def left_copy(group, mat, raw=False):
        return pltpu.make_async_remote_copy(
            src_ref=own.at[group * count + mat] if raw else from_right.at[group, mat],
            dst_ref=from_right.at[group, mat],
            send_sem=left_send.at[group, mat],
            recv_sem=left_recv.at[group, mat],
            device_id={"replica": rep - 1},
        )

    def gather_copy(mat, slot):
        return pltpu.make_async_remote_copy(
            src_ref=outgoing.at[mat],
            dst_ref=gathered.at[slot],
            send_sem=gather_send.at[mat],
            recv_sem=gather_recv.at[slot],
            device_id={"fsdp": owner_of(mat)},
        )

    def return_copy(mat, slot):
        return pltpu.make_async_remote_copy(
            src_ref=finished.at[slot],
            dst_ref=returned.at[mat],
            send_sem=return_send.at[slot],
            recv_sem=return_recv.at[mat],
            device_id={"fsdp": slot},
        )

    def stored_copy(mat):
        return pltpu.make_async_copy(stored.at[mat], stored_out.at[mat], out_sem.at[0, mat])

    def orth_copy(mat):
        return pltpu.make_async_copy(returned.at[mat], orth_out.at[mat], out_sem.at[1, mat])

    def send_raw(mat):
        @pl.when(rep == 0)
        def _():
            for group in range(n_rep - 1, 0, -1):
                right_copy(group, mat, raw=True).start()

        @pl.when(rep == n_rep - 1)
        def _():
            for group in range(n_rep - 1):
                left_copy(group, mat, raw=True).start()

    def forward(mat):
        for step in range(n_rep - 1):
            high, low = n_rep - 1 - step, step

            @pl.when((rep > 0) & (rep < high))
            def _():
                right_copy(high, mat).wait_recv()
                from_left[high, mat] = add_rows(
                    from_left[high, mat], own[high * count + mat]
                ).astype(jnp.bfloat16)
                right_copy(high, mat).start()

            @pl.when((rep < n_rep - 1) & (rep > low))
            def _():
                left_copy(low, mat).wait_recv()
                from_right[low, mat] = add_rows(
                    from_right[low, mat], own[low * count + mat]
                ).astype(jnp.bfloat16)
                left_copy(low, mat).start()

    def finish_sum(mat):
        total[...] = own[rep * count + mat].astype(jnp.float32)

        @pl.when(rep > 0)
        def _():
            right_copy(rep, mat).wait_recv()
            total[...] += from_left[rep, mat].astype(jnp.float32)

        @pl.when(rep < n_rep - 1)
        def _():
            left_copy(rep, mat).wait_recv()
            total[...] += from_right[rep, mat].astype(jnp.float32)

        summed = total[...]
        kept = (coef_ref[0, mat] * old[mat].astype(jnp.float32) + coef_ref[1, mat] * summed).astype(
            jnp.bfloat16
        )
        stored[mat] = kept
        stored_copy(mat).start()
        outgoing[mat] = (summed + MOMENTUM_DECAY * kept.astype(jnp.float32)).astype(jnp.bfloat16)

        @pl.when(me == owner_of(mat))
        def _():
            gathered[me] = outgoing[mat]

        @pl.when(me != owner_of(mat))
        def _():
            gather_copy(mat, me).start()

    def orthogonalize():
        @pl.loop(1, n_fsdp)
        def _(step):
            gather_copy(mine, lax.rem(me + step, n_fsdp)).wait_recv()

        scaled = gathered[...].astype(jnp.float32)
        frobenius = jnp.sqrt(jnp.sum(scaled * scaled))
        inverse = 1.0 / (frobenius + EPSILON)
        iterate[...] = (
            (scaled * inverse).reshape(n_fsdp * row_count, col_count).astype(jnp.bfloat16)
        )

        def newton(last):
            held = iterate[...]
            gram[...] = lax.dot_general(
                held, held, (((1,), (1,)), ((), ())), preferred_element_type=jnp.float32
            ).astype(jnp.bfloat16)
            square = jnp.dot(gram[...], gram[...], preferred_element_type=jnp.float32)
            poly[...] = (
                COEFF_CUBIC * gram[...].astype(jnp.float32) + COEFF_QUINTIC * square
            ).astype(jnp.bfloat16)
            product = jnp.dot(poly[...], iterate[...], preferred_element_type=jnp.float32)
            result = COEFF_LINEAR * iterate[...].astype(jnp.float32) + product
            if last:
                finished[...] = result.reshape(n_fsdp, row_count, col_count).astype(jnp.bfloat16)
            else:
                iterate[...] = result.astype(jnp.bfloat16)

        for turn in range(ITERS):
            newton(turn == ITERS - 1)

        @pl.loop(1, n_fsdp)
        def _(step):
            return_copy(mine, lax.rem(me + step, n_fsdp)).start()

        returned[mine] = finished[me]

    send_raw(0)

    @pl.loop(0, count + 1)
    def _(turn):
        @pl.when(turn < count - 1)
        def _():
            send_raw(turn + 1)

        @pl.when(turn < count)
        def _():
            forward(turn)
            finish_sum(turn)

        @pl.when(is_owner & (turn == turn_of_mine))
        def _():
            orthogonalize()

    @pl.loop(0, count)
    def _(mat):
        @pl.when(me != owner_of(mat))
        def _():
            return_copy(mat, me).wait_recv()

        orth_copy(mat).start()

    @pl.loop(0, count)
    def _(mat):
        for group in range(n_rep):

            @pl.when(rep < group)
            def _():
                right_copy(group, mat).wait_send()

            @pl.when(rep > group)
            def _():
                left_copy(group, mat).wait_send()

        @pl.when(me != owner_of(mat))
        def _():
            gather_copy(mat, me).wait_send()

        stored_copy(mat).wait()
        orth_copy(mat).wait()

    @pl.when(is_owner)
    def _():
        @pl.loop(1, n_fsdp)
        def _(step):
            return_copy(mine, lax.rem(me + step, n_fsdp)).wait_send()


def fused_sum_and_orthogonalize(n_rep, n_fsdp, coefs, grads, momentum):
    count, row_count, col_count = momentum.shape
    all_rows = n_fsdp * row_count
    block = (row_count, col_count)
    half = jnp.bfloat16
    shape = jax.ShapeDtypeStruct(momentum.shape, half)
    dma = pltpu.SemaphoreType.DMA
    return pl.pallas_call(
        functools.partial(fused_kernel, n_rep, n_fsdp, count),
        out_shape=(shape, shape),
        in_specs=[
            pl.BlockSpec(memory_space=pltpu.SMEM),
            pl.BlockSpec(memory_space=pl.ANY),
            pl.BlockSpec(memory_space=pl.ANY),
        ],
        out_specs=(pl.BlockSpec(memory_space=pl.ANY), pl.BlockSpec(memory_space=pl.ANY)),
        scratch_shapes=[
            pltpu.VMEM((n_rep * count, *block), half),
            pltpu.VMEM((count, *block), half),
            pltpu.VMEM((n_rep, count, *block), half),
            pltpu.VMEM((n_rep, count, *block), half),
            pltpu.VMEM(block, jnp.float32),
            pltpu.VMEM((count, *block), half),
            pltpu.VMEM((count, *block), half),
            pltpu.VMEM((n_fsdp, *block), half),
            pltpu.VMEM((all_rows, col_count), half),
            pltpu.VMEM((all_rows, all_rows), half),
            pltpu.VMEM((all_rows, all_rows), half),
            pltpu.VMEM((n_fsdp, *block), half),
            pltpu.VMEM((count, *block), half),
            dma((2,)),
            dma((n_rep, count)),
            dma((n_rep, count)),
            dma((n_rep, count)),
            dma((n_rep, count)),
            dma((count,)),
            dma((n_fsdp,)),
            dma((n_fsdp,)),
            dma((count,)),
            dma((2, count)),
        ],
        compiler_params=pltpu.CompilerParams(
            collective_id=0, has_side_effects=True, vmem_limit_bytes=KERNEL_VMEM
        ),
        name="sum_and_orthogonalize",
    )(coefs, grads, momentum)


def finish_kernel(coef_ref, stored_ref, orth_ref, weight_ref, momentum_out, update_out, weight_out):
    mat = pl.program_id(0)
    momentum_out[...] = stored_ref[...]
    orth = orth_ref[...].astype(jnp.float32)
    update_out[...] = (coef_ref[2, mat] * orth).astype(jnp.bfloat16)
    weight_out[...] = (
        coef_ref[3, mat] * weight_ref[...].astype(jnp.float32) - coef_ref[4, mat] * orth
    ).astype(jnp.bfloat16)


def finish(coefs, stored, orth, weight):
    count, row_count, col_count = weight.shape
    block = pl.BlockSpec((1, row_count, col_count), lambda mat: (mat, 0, 0))
    shape = jax.ShapeDtypeStruct(weight.shape, jnp.bfloat16)
    return pl.pallas_call(
        finish_kernel,
        grid=(count,),
        out_shape=(shape, shape, shape),
        in_specs=[pl.BlockSpec(memory_space=pltpu.SMEM), block, block, block],
        out_specs=(block, block, block),
        name="finish",
    )(coefs, stored, orth, weight)


def coefficients(active, update_scale):
    on = active.astype(jnp.float32)
    return jnp.stack(
        [
            jnp.where(active, MOMENTUM_DECAY, 1.0),
            on,
            update_scale * on,
            jnp.where(active, 1.0 - LEARN_RATE * DECAY_RATE, 1.0),
            LEARN_RATE * update_scale * on,
        ]
    )


def by_collectives(grads, momentum, weight, active, update_scale):
    groups = lax.axis_size("fsdp")
    summed = lax.psum_scatter(
        grads[0], "replica", scatter_dimension=0, tiled=True
    ).astype(jnp.float32)
    local_count, row_count, col_count = momentum.shape
    keep_mask = active[:, None, None]
    old_momentum = momentum.astype(jnp.float32)
    new_momentum = jnp.where(
        keep_mask, MOMENTUM_DECAY * old_momentum + summed, old_momentum
    ).astype(jnp.bfloat16)
    stored = lax.optimization_barrier(new_momentum)
    outgoing = (summed + MOMENTUM_DECAY * stored.astype(jnp.float32)).astype(jnp.bfloat16)
    slots = -(-local_count // groups)
    padding = slots * groups - local_count
    packed = jnp.pad(outgoing, ((0, padding), (0, 0), (0, 0)))
    received = lax.all_to_all(packed, "fsdp", split_axis=0, concat_axis=1, tiled=True)
    orthogonal = newton_blocks(received)
    returned = lax.all_to_all(orthogonal, "fsdp", split_axis=1, concat_axis=0, tiled=True)
    restored = jnp.where(keep_mask, returned[:local_count].astype(jnp.float32), 0.0)
    update = (update_scale * restored).astype(jnp.bfloat16)
    old_weight = weight.astype(jnp.float32)
    stepped = old_weight * (1.0 - LEARN_RATE * DECAY_RATE) - LEARN_RATE * update_scale * restored
    new_weight = jnp.where(keep_mask, stepped, old_weight).astype(jnp.bfloat16)
    return (new_momentum, update, new_weight)


def on_device(grads, momentum, weight, owners):
    n_fsdp = lax.axis_size("fsdp")
    n_rep = lax.axis_size("replica")
    count, row_count, col_count = momentum.shape
    update_scale = UPDATE_RATIO * math.sqrt(max(row_count * n_fsdp, col_count))
    offset = lax.axis_index("replica") * count
    active = lax.dynamic_slice_in_dim(owners, offset, count) < n_fsdp
    held_bytes = 2 * row_count * col_count * (3 * n_rep * count + 4 * count + 4 * n_fsdp)
    fits = held_bytes * 2 < KERNEL_VMEM * 3 // 2 and row_count % ROW_TILE == 0
    if not fits or n_fsdp % 2 or count > n_fsdp or n_rep < 2 or count < 3:
        return by_collectives(grads, momentum, weight, active, update_scale)
    coefs = coefficients(active, update_scale)
    stored, orth = fused_sum_and_orthogonalize(n_rep, n_fsdp, coefs, grads[0], momentum)
    return finish(coefs, stored, orth, weight)


def solution(mesh):
    in_specs = (
        P("replica", None, "fsdp", None),
        P("replica", "fsdp", None),
        P("replica", "fsdp", None),
        P(),
    )
    out_specs = (P("replica", "fsdp", None), P("replica", "fsdp", None), P("replica", "fsdp", None))
    return jax.shard_map(
        on_device, mesh=mesh, in_specs=in_specs, out_specs=out_specs, check_vma=False
    )
```

time: 223 us -> 111 us (0.50); the launches traced: 219 us -> 110 us
  Pallas kernels: 0 us -> 108 us
  waiting for transfers between devices: 102 us -> 0 us
  blocking collectives: 38 us -> 0 us
  matrix products: 35.3 us -> 0 us
  local copies, waits for them, and re-layouts: 17.9 us -> 0.6 us
  between operations: 14.1 us -> 0.64 us
  starting transfers between devices: 5.68 us -> 0 us
  other arithmetic: 6.23 us -> 0.75 us
    pallas_call x0 -> x2, Pallas kernels: none -> 108 us  [the longest x1 104 us: fused_sum_and_orthogonalize(): pl.pallas_call(functools.partial(fused_kernel, n_rep, n_fsdp, count), out...]
    reduce_scatter x1 -> x0, waiting for transfers between devices: 71.5 us -> none  [on_device(): lax.psum_scatter(grads[0].astype(jnp.float32).astype(jnp.bfloat16), 'repl...]
    all_to_all x1 -> x0, blocking collectives: 38 us -> none  [on_device(): lax.all_to_all(packed, 'fsdp', split_axis=0, concat_axis=2, tiled=True)]
    dot_general x6 -> x0, matrix products: 35.3 us -> none  [the longest x2 21.1 us: newton_blocks(): jnp.einsum('cij,cjk->cik', poly_term, iterate, preferred_element_type=jnp...]
    all_to_all x1 -> x0, waiting for transfers between devices: 30.1 us -> none  [on_device(): lax.all_to_all(orthogonal, 'fsdp', split_axis=2, concat_axis=0, tiled=True)]
    unnamed x14 -> x0, local copies, waits for them, and re-layouts: 7.75 us -> none
    broadcast_in_dim x1 -> x0, local copies, waits for them, and re-layouts: 6.35 us -> none  [newton_items(): return newton_blocks(received[0])[None]]
    all_to_all x1 -> x0, starting transfers between devices: 5.64 us -> none  [on_device(): lax.all_to_all(orthogonal, 'fsdp', split_axis=2, concat_axis=0, tiled=True)]
  transfers between devices with their start and end apart: 2 -> 0, of which waited for: 2 -> 0; matrix products, arithmetic and copies ran while one was open for 1% -> 0% of each run, Pallas kernels for 0% -> 0%
where the time goes in v1:
time: 111 us; the launch traced here: 110 us
  Pallas kernels  108 us (97%)
    pallas_call x1, Pallas kernels, fused_sum_and_orthogonalize(): pl.pallas_call(functools.partial(fused_kernel, n_rep, n_fsdp, count), out...  104 us
    pallas_call x1, Pallas kernels, finish(): pl.pallas_call(finish_kernel, grid=(count,), out_shape=(shape, shape, sha...  4.76 us

profile of v1, /device:TPU:1, one launch (start us, length us, event | category | flops | bytes accessed | tf_op | source)
XLA Modules:
  0.0 110.4 jit_solution(2487626439151729867)
XLA Ops:
  0.6 0.7 select_bitcast_fusion
  1.4 0.6 stack.27.coef_ref
  2.0 103.7 %sum_and_orthogonalize.1 = (bf16[5,88,1024]{2,1,0:T(8,128)(2,1)}, bf16[5,88,1024]{2,1,0:T(8,128)(2,1)}) custom-call(f32[5,5]{1,0:T(8,128)} %stack.27.coef_ref, bf16[20,88,1024]{2,1,0:T(8,128)(2,1)} %bitcast.11, bf16[5,88,1024]{2,1,0:T(8,128)(2,1)} %momentum_ref.1), custom_call_target="tpu_custom_call" | custom-call | tf_op jit(solution)/shard_map/sum_and_orthogonalize/pallas_call | solution.py:318
  105.7 4.8 %finish.1 = (bf16[5,88,1024]{2,1,0:T(8,128)(2,1)}, bf16[5,88,1024]{2,1,0:T(8,128)(2,1)}, bf16[5,88,1024]{2,1,0:T(8,128)(2,1)}) custom-call(f32[5,5]{1,0:T(8,128)} %stack.27.coef_ref, bf16[5,88,1024]{2,1,0:T(8,128)(2,1)} %get-tuple-element.5.stored_ref, bf16[5,88,1024]{2,1,0:T(8,128)(2,1)} %get-tuple-element.6.orth_ref, bf16[5,88,1024]{2,1,0:T(8,128)(2,1)} %weight_ref.1), custom_call_target="tpu_custom_call" | custom-call | tf_op jit(solution)/shard_map/finish/pallas_call | solution.py:373
  (2 shorter events, 0.0 us)

commit v2 on v1

v2 whole, which is shorter than its diff:
```python
import functools
import math

import jax
import jax.numpy as jnp
from jax import lax
from jax.experimental import pallas as pl
from jax.experimental.pallas import tpu as pltpu
from jax.sharding import PartitionSpec as P

ITERS = 2
ROW_TILE = 8
KERNEL_VMEM = 56 * 1024 * 1024
PARTS = 4
LOOK_AHEAD = 4
GATHER_TURNS = 3


EPSILON = 1e-07
COEFF_LINEAR = 3.4445
COEFF_CUBIC = -4.775
COEFF_QUINTIC = 2.0315
MOMENTUM_DECAY = 0.95
LEARN_RATE = 0.02
DECAY_RATE = 0.1
UPDATE_RATIO = 0.2


def newton_blocks(blocks):
    scaled = blocks.astype(jnp.float32)
    frobenius = jnp.sqrt(jnp.sum(scaled * scaled, axis=(1, 2), keepdims=True))
    iterate = lax.optimization_barrier((scaled / (frobenius + EPSILON)).astype(jnp.bfloat16))
    for turn in range(ITERS):
        gram_matrix = jnp.einsum(
            "cik,cjk->cij", iterate, iterate, preferred_element_type=jnp.float32
        ).astype(jnp.bfloat16)
        gram_matrix = lax.optimization_barrier(gram_matrix)
        gram_square = jnp.einsum(
            "cij,cjk->cik", gram_matrix, gram_matrix, preferred_element_type=jnp.float32
        )
        poly_term = (
            COEFF_CUBIC * gram_matrix.astype(jnp.float32) + COEFF_QUINTIC * gram_square
        ).astype(jnp.bfloat16)
        product = jnp.einsum("cij,cjk->cik", poly_term, iterate, preferred_element_type=jnp.float32)
        iterate = (COEFF_LINEAR * iterate.astype(jnp.float32) + product).astype(jnp.bfloat16)
        iterate = lax.optimization_barrier(iterate)
    return iterate


def add_rows(left, right):
    return left.astype(jnp.float32) + right.astype(jnp.float32)


def fused_kernel(
    n_rep,
    n_fsdp,
    count,
    owners_ref,
    grads_ref,
    momentum_ref,
    stored_out,
    orth_out,
    own,
    old,
    from_left,
    from_right,
    total,
    stored,
    outgoing,
    gathered,
    iterate,
    gram,
    poly,
    finished,
    returned,
    load_sem,
    right_send,
    right_recv,
    left_send,
    left_recv,
    gather_send,
    gather_recv,
    return_send,
    return_recv,
    out_sem,
):
    rep = lax.axis_index("replica")
    me = lax.axis_index("fsdp")
    row_count, col_count = own.shape[1:]
    width = col_count // PARTS
    units = count * PARTS
    chips = n_fsdp // 2
    early_count = count - 2
    chip, core = me // 2, lax.rem(me, 2)
    partner = me + 1 - 2 * core

    has_early = (core == 1) & (chip < early_count)

    def early_owner(mat):
        return mat * 2 + 1

    def columns(part):
        return pl.ds(pl.multiple_of(part * width, 128), width)

    load_grads = pltpu.make_async_copy(grads_ref, own, load_sem.at[0])
    load_old = pltpu.make_async_copy(momentum_ref, old, load_sem.at[1])
    load_grads.start()
    load_old.start()

    barrier = pltpu.get_barrier_semaphore()
    for step in range(1, n_fsdp):
        pl.semaphore_signal(barrier, inc=1, device_id={"fsdp": lax.rem(me + step, n_fsdp)})

    @pl.when(rep > 0)
    def _():
        pl.semaphore_signal(barrier, inc=1, device_id={"replica": rep - 1})

    @pl.when(rep < n_rep - 1)
    def _():
        pl.semaphore_signal(barrier, inc=1, device_id={"replica": rep + 1})

    inner = (rep > 0) & (rep < n_rep - 1)
    pl.semaphore_wait(barrier, jnp.where(inner, n_fsdp + 1, n_fsdp))
    load_grads.wait()
    load_old.wait()

    def right_copy(group, unit, raw=False):
        mat, cols = unit // PARTS, columns(lax.rem(unit, PARTS))
        held = own.at[group * count + mat] if raw else from_left.at[group, mat]
        return pltpu.make_async_remote_copy(
            src_ref=held.at[:, cols],
            dst_ref=from_left.at[group, mat, :, cols],
            send_sem=right_send.at[group, unit],
            recv_sem=right_recv.at[group, unit],
            device_id={"replica": rep + 1},
        )

    def left_copy(group, unit, raw=False):
        mat, cols = unit // PARTS, columns(lax.rem(unit, PARTS))
        held = own.at[group * count + mat] if raw else from_right.at[group, mat]
        return pltpu.make_async_remote_copy(
            src_ref=held.at[:, cols],
            dst_ref=from_right.at[group, mat, :, cols],
            send_sem=left_send.at[group, unit],
            recv_sem=left_recv.at[group, unit],
            device_id={"replica": rep - 1},
        )

    def gather_copy(unit, job, slot, target, place):
        mat, part = unit // PARTS, lax.rem(unit, PARTS)
        cols = columns(part)
        return pltpu.make_async_remote_copy(
            src_ref=outgoing.at[mat, :, cols],
            dst_ref=gathered.at[job, slot, :, cols],
            send_sem=gather_send.at[unit, place],
            recv_sem=gather_recv.at[job, slot, part],
            device_id={"fsdp": target},
        )

    def return_copy(job, mat, slot):
        return pltpu.make_async_remote_copy(
            src_ref=finished.at[job, slot],
            dst_ref=returned.at[mat],
            send_sem=return_send.at[job, slot],
            recv_sem=return_recv.at[mat],
            device_id={"fsdp": slot},
        )

    def stored_copy(mat):
        return pltpu.make_async_copy(stored.at[mat], stored_out.at[mat], out_sem.at[0, mat])

    def orth_copy(mat):
        return pltpu.make_async_copy(returned.at[mat], orth_out.at[mat], out_sem.at[1, mat])

    def send_raw(unit):
        @pl.when(rep == 0)
        def _():
            for group in range(n_rep - 1, 0, -1):
                right_copy(group, unit, raw=True).start()

        @pl.when(rep == n_rep - 1)
        def _():
            for group in range(n_rep - 1):
                left_copy(group, unit, raw=True).start()

    def forward(unit):
        mat, cols = unit // PARTS, columns(lax.rem(unit, PARTS))
        for step in range(n_rep - 1):
            high, low = n_rep - 1 - step, step

            @pl.when((rep > 0) & (rep < high))
            def _():
                right_copy(high, unit).wait_recv()
                from_left[high, mat, :, cols] = add_rows(
                    from_left[high, mat, :, cols], own[high * count + mat, :, cols]
                ).astype(jnp.bfloat16)
                right_copy(high, unit).start()

            @pl.when((rep < n_rep - 1) & (rep > low))
            def _():
                left_copy(low, unit).wait_recv()
                from_right[low, mat, :, cols] = add_rows(
                    from_right[low, mat, :, cols], own[low * count + mat, :, cols]
                ).astype(jnp.bfloat16)
                left_copy(low, unit).start()

    def each_gather(unit, act):
        mat = unit // PARTS
        late_core = mat - early_count

        @pl.when((mat < early_count) & (me != early_owner(mat)))
        def _():
            act(gather_copy(unit, 0, me, early_owner(mat), 0))

        @pl.when(mat >= early_count)
        def _():
            for step in range(1, chips):
                target = lax.rem(chip + step, chips) * 2 + late_core
                act(gather_copy(unit, 1, me, target, step))

            @pl.when(core != late_core)
            def _():
                act(gather_copy(unit, 1, me, partner, 0))

    def finish_sum(unit):
        mat, cols = unit // PARTS, columns(lax.rem(unit, PARTS))
        total[...] = own[rep * count + mat, :, cols].astype(jnp.float32)

        @pl.when(rep > 0)
        def _():
            right_copy(rep, unit).wait_recv()
            total[...] += from_left[rep, mat, :, cols].astype(jnp.float32)

        @pl.when(rep < n_rep - 1)
        def _():
            left_copy(rep, unit).wait_recv()
            total[...] += from_right[rep, mat, :, cols].astype(jnp.float32)

        summed = total[...]
        active = owners_ref[rep * count + mat] < n_fsdp
        decay = jnp.where(active, jnp.float32(MOMENTUM_DECAY), jnp.float32(1.0))
        gain = jnp.where(active, jnp.float32(1.0), jnp.float32(0.0))
        kept = (decay * old[mat, :, cols].astype(jnp.float32) + gain * summed).astype(jnp.bfloat16)
        stored[mat, :, cols] = kept
        nesterov = (summed + MOMENTUM_DECAY * kept.astype(jnp.float32)).astype(jnp.bfloat16)
        outgoing[mat, :, cols] = nesterov

        @pl.when((mat < early_count) & (me == early_owner(mat)))
        def _():
            gathered[0, me, :, cols] = nesterov

        @pl.when((mat >= early_count) & (core == mat - early_count))
        def _():
            gathered[1, me, :, cols] = nesterov

        each_gather(unit, lambda copy: copy.start())

        @pl.when(lax.rem(unit, PARTS) == PARTS - 1)
        def _():
            stored_copy(mat).start()

    def make_gram():
        held = iterate[...]
        gram[...] = lax.dot_general(
            held, held, (((1,), (1,)), ((), ())), preferred_element_type=jnp.float32
        ).astype(jnp.bfloat16)

    def make_poly(rows):
        square = jnp.dot(gram[rows, :], gram[...], preferred_element_type=jnp.float32)
        poly[rows, :] = (
            COEFF_CUBIC * gram[rows, :].astype(jnp.float32) + COEFF_QUINTIC * square
        ).astype(jnp.bfloat16)

    def apply_poly(rows):
        product = jnp.dot(poly[rows, :], iterate[...], preferred_element_type=jnp.float32)
        return COEFF_LINEAR * iterate[rows, :].astype(jnp.float32) + product

    def orthogonalize(job, mat):
        @pl.loop(1, n_fsdp)
        def _(step):
            for part in range(PARTS):
                unit = mat * PARTS + part
                gather_copy(unit, job, lax.rem(me + step, n_fsdp), me, 0).wait_recv()

        scaled = gathered[job].astype(jnp.float32)
        frobenius = jnp.sqrt(jnp.sum(scaled * scaled))
        inverse = 1.0 / (frobenius + EPSILON)
        iterate[...] = (
            (scaled * inverse).reshape(n_fsdp * row_count, col_count).astype(jnp.bfloat16)
        )
        whole = pl.ds(0, n_fsdp * row_count)
        for turn in range(ITERS - 1):
            make_gram()
            make_poly(whole)
            iterate[...] = apply_poly(whole).astype(jnp.bfloat16)
        make_gram()

        @pl.when(job == 0)
        def _():
            make_poly(whole)
            finished[0] = (
                apply_poly(whole).reshape(n_fsdp, row_count, col_count).astype(jnp.bfloat16)
            )

            @pl.loop(1, n_fsdp)
            def _(step):
                return_copy(0, mat, lax.rem(me + step, n_fsdp)).start()

            returned[mat] = finished[0, me]

        @pl.when(job == 1)
        def _():
            pair = pl.ds(pl.multiple_of(chip * (2 * row_count), 16), 2 * row_count)
            make_poly(pair)
            rows = apply_poly(pair).reshape(2, row_count, col_count).astype(jnp.bfloat16)
            finished[1, pl.ds(chip * 2, 2)] = rows
            return_copy(1, mat, partner).start()
            returned[mat] = finished[1, me]

    ahead = LOOK_AHEAD
    for unit in range(ahead):
        send_raw(unit)

    @pl.loop(0, units)
    def _(turn):
        @pl.when(turn < units - ahead)
        def _():
            send_raw(turn + ahead)

        forward(turn)
        finish_sum(turn)
        last = turn == units - 1
        early = has_early & (turn == (chip + 1) * PARTS - 1 + GATHER_TURNS)

        @pl.when(last | early)
        def _():
            job = jnp.where(last, 1, 0)
            orthogonalize(job, jnp.where(last, early_count + core, chip))

    @pl.loop(0, count)
    def _(mat):
        held_here = jnp.where(
            mat < early_count, me == early_owner(mat), core == mat - early_count
        )

        @pl.when(jnp.logical_not(held_here))
        def _():
            return_copy(0, mat, me).wait_recv()

        orth_copy(mat).start()

    @pl.loop(0, units)
    def _(unit):
        for group in range(n_rep):

            @pl.when(rep < group)
            def _():
                right_copy(group, unit).wait_send()

            @pl.when(rep > group)
            def _():
                left_copy(group, unit).wait_send()

        each_gather(unit, lambda copy: copy.wait_send())

    @pl.loop(0, count)
    def _(mat):
        stored_copy(mat).wait()
        orth_copy(mat).wait()

    @pl.when(has_early)
    def _():
        @pl.loop(1, n_fsdp)
        def _(step):
            return_copy(0, chip, lax.rem(me + step, n_fsdp)).wait_send()

    return_copy(1, early_count + core, partner).wait_send()


def fused_sum_and_orthogonalize(n_rep, n_fsdp, owners, grads, momentum):
    count, row_count, col_count = momentum.shape
    all_rows = n_fsdp * row_count
    units = count * PARTS
    block = (row_count, col_count)
    half = jnp.bfloat16
    shape = jax.ShapeDtypeStruct(momentum.shape, half)
    dma = pltpu.SemaphoreType.DMA
    return pl.pallas_call(
        functools.partial(fused_kernel, n_rep, n_fsdp, count),
        out_shape=(shape, shape),
        in_specs=[
            pl.BlockSpec(memory_space=pltpu.SMEM),
            pl.BlockSpec(memory_space=pl.ANY),
            pl.BlockSpec(memory_space=pl.ANY),
        ],
        out_specs=(pl.BlockSpec(memory_space=pl.ANY), pl.BlockSpec(memory_space=pl.ANY)),
        scratch_shapes=[
            pltpu.VMEM((n_rep * count, *block), half),
            pltpu.VMEM((count, *block), half),
            pltpu.VMEM((n_rep, count, *block), half),
            pltpu.VMEM((n_rep, count, *block), half),
            pltpu.VMEM((row_count, col_count // PARTS), jnp.float32),
            pltpu.VMEM((count, *block), half),
            pltpu.VMEM((count, *block), half),
            pltpu.VMEM((2, n_fsdp, *block), half),
            pltpu.VMEM((all_rows, col_count), half),
            pltpu.VMEM((all_rows, all_rows), half),
            pltpu.VMEM((all_rows, all_rows), half),
            pltpu.VMEM((2, n_fsdp, *block), half),
            pltpu.VMEM((count, *block), half),
            dma((2,)),
            dma((n_rep, units)),
            dma((n_rep, units)),
            dma((n_rep, units)),
            dma((n_rep, units)),
            dma((units, n_fsdp // 2)),
            dma((2, n_fsdp, PARTS)),
            dma((2, n_fsdp)),
            dma((count,)),
            dma((2, count)),
        ],
        compiler_params=pltpu.CompilerParams(
            collective_id=0, has_side_effects=True, vmem_limit_bytes=KERNEL_VMEM
        ),
        name="sum_and_orthogonalize",
    )(owners, grads, momentum)


def finish_kernel(
    n_fsdp,
    update_scale,
    owners_ref,
    stored_ref,
    orth_ref,
    weight_ref,
    momentum_out,
    update_out,
    weight_out,
    stored,
    orth,
    weight,
    update,
    stepped,
    in_sem,
    out_sem,
):
    count = weight_ref.shape[0]
    offset = lax.axis_index("replica") * count
    loads, stores = [], []
    for mat in range(count):
        loads.append(
            [
                pltpu.make_async_copy(source.at[mat], held.at[mat], in_sem.at[place, mat])
                for place, (source, held) in enumerate(
                    ((orth_ref, orth), (weight_ref, weight), (stored_ref, stored))
                )
            ]
        )
        for copy in loads[-1]:
            copy.start()
    for mat in range(count):
        for copy in loads[mat]:
            copy.wait()
        on = jnp.where(owners_ref[offset + mat] < n_fsdp, jnp.float32(1.0), jnp.float32(0.0))
        held = orth[mat].astype(jnp.float32)
        update[mat] = ((update_scale * on) * held).astype(jnp.bfloat16)
        stepped[mat] = (
            weight[mat].astype(jnp.float32) * (1.0 - (LEARN_RATE * DECAY_RATE) * on)
            - (LEARN_RATE * update_scale * on) * held
        ).astype(jnp.bfloat16)
        for place, (held, target) in enumerate(
            ((stored, momentum_out), (update, update_out), (stepped, weight_out))
        ):
            copy = pltpu.make_async_copy(held.at[mat], target.at[mat], out_sem.at[place, mat])
            copy.start()
            stores.append(copy)
    for copy in stores:
        copy.wait()


def finish(n_fsdp, update_scale, owners, stored, orth, weight):
    count = weight.shape[0]
    anywhere = pl.BlockSpec(memory_space=pl.ANY)
    shape = jax.ShapeDtypeStruct(weight.shape, jnp.bfloat16)
    return pl.pallas_call(
        functools.partial(finish_kernel, n_fsdp, update_scale),
        out_shape=(shape, shape, shape),
        in_specs=[pl.BlockSpec(memory_space=pltpu.SMEM), anywhere, anywhere, anywhere],
        out_specs=(anywhere, anywhere, anywhere),
        scratch_shapes=[pltpu.VMEM(weight.shape, jnp.bfloat16)] * 5
        + [pltpu.SemaphoreType.DMA((3, count))] * 2,
        compiler_params=pltpu.CompilerParams(vmem_limit_bytes=KERNEL_VMEM),
        name="finish",
    )(owners, stored, orth, weight)


def by_collectives(grads, momentum, weight, active, update_scale):
    groups = lax.axis_size("fsdp")
    summed = lax.psum_scatter(
        grads[0], "replica", scatter_dimension=0, tiled=True
    ).astype(jnp.float32)
    local_count, row_count, col_count = momentum.shape
    keep_mask = active[:, None, None]
    old_momentum = momentum.astype(jnp.float32)
    new_momentum = jnp.where(
        keep_mask, MOMENTUM_DECAY * old_momentum + summed, old_momentum
    ).astype(jnp.bfloat16)
    stored = lax.optimization_barrier(new_momentum)
    outgoing = (summed + MOMENTUM_DECAY * stored.astype(jnp.float32)).astype(jnp.bfloat16)
    slots = -(-local_count // groups)
    padding = slots * groups - local_count
    packed = jnp.pad(outgoing, ((0, padding), (0, 0), (0, 0)))
    received = lax.all_to_all(packed, "fsdp", split_axis=0, concat_axis=1, tiled=True)
    orthogonal = newton_blocks(received)
    returned = lax.all_to_all(orthogonal, "fsdp", split_axis=1, concat_axis=0, tiled=True)
    restored = jnp.where(keep_mask, returned[:local_count].astype(jnp.float32), 0.0)
    update = (update_scale * restored).astype(jnp.bfloat16)
    old_weight = weight.astype(jnp.float32)
    stepped = old_weight * (1.0 - LEARN_RATE * DECAY_RATE) - LEARN_RATE * update_scale * restored
    new_weight = jnp.where(keep_mask, stepped, old_weight).astype(jnp.bfloat16)
    return (new_momentum, update, new_weight)


def on_device(grads, momentum, weight, owners):
    n_fsdp = lax.axis_size("fsdp")
    n_rep = lax.axis_size("replica")
    count, row_count, col_count = momentum.shape
    update_scale = UPDATE_RATIO * math.sqrt(max(row_count * n_fsdp, col_count))
    offset = lax.axis_index("replica") * count
    active = lax.dynamic_slice_in_dim(owners, offset, count) < n_fsdp
    held_bytes = 2 * row_count * col_count * (3 * n_rep * count + 4 * count + 8 * n_fsdp)
    fits = held_bytes < KERNEL_VMEM // 2 and row_count % ROW_TILE == 0
    fits = fits and col_count % (128 * PARTS) == 0
    if not fits or n_fsdp % 2 or n_rep < 2 or not 3 <= count <= n_fsdp // 2 + 2:
        return by_collectives(grads, momentum, weight, active, update_scale)
    stored, orth = fused_sum_and_orthogonalize(n_rep, n_fsdp, owners, grads[0], momentum)
    return finish(n_fsdp, update_scale, owners, stored, orth, weight)


def solution(mesh):
    in_specs = (
        P("replica", None, "fsdp", None),
        P("replica", "fsdp", None),
        P("replica", "fsdp", None),
        P(),
    )
    out_specs = (P("replica", "fsdp", None), P("replica", "fsdp", None), P("replica", "fsdp", None))
    return jax.shard_map(
        on_device, mesh=mesh, in_specs=in_specs, out_specs=out_specs, check_vma=False
    )
```

time: 111 us -> 171 us (1.54)
  Pallas kernels: 108 us -> 170 us
    pallas_call x1, Pallas kernels: 104 us -> 166 us  [fused_sum_and_orthogonalize(): pl.pallas_call(functools.partial(fused_kernel, n_rep, n_fsdp, count), out...]
where the time goes in v2:
time: 171 us; the launch traced here: 170 us
  Pallas kernels  170 us (99%)
    pallas_call x1, Pallas kernels, fused_sum_and_orthogonalize(): pl.pallas_call(functools.partial(fused_kernel, n_rep, n_fsdp, count), out...  166 us
    pallas_call x1, Pallas kernels, finish(): pl.pallas_call(functools.partial(finish_kernel, n_fsdp, update_scale), ou...  3.55 us

profile of v2, /device:TPU:1, one launch (start us, length us, event | category | flops | bytes accessed | tf_op | source)
XLA Modules:
  0.0 170.3 jit_solution(14776865897137567951)
XLA Ops:
  0.6 166.1 %sum_and_orthogonalize.1 = (bf16[5,88,1024]{2,1,0:T(8,128)(2,1)}, bf16[5,88,1024]{2,1,0:T(8,128)(2,1)}) custom-call(s32[20]{0:T(128)} %owners_ref.3, bf16[20,88,1024]{2,1,0:T(8,128)(2,1)} %bitcast.1, bf16[5,88,1024]{2,1,0:T(8,128)(2,1)} %momentum_ref.1), custom_call_target="tpu_custom_call" | custom-call | tf_op jit(solution)/shard_map/sum_and_orthogonalize/pallas_call | solution.py:388
  166.7 3.6 %finish.1 = (bf16[5,88,1024]{2,1,0:T(8,128)(2,1)}, bf16[5,88,1024]{2,1,0:T(8,128)(2,1)}, bf16[5,88,1024]{2,1,0:T(8,128)(2,1)}) custom-call(s32[20]{0:T(128)} %owners_ref.3, bf16[5,88,1024]{2,1,0:T(8,128)(2,1)} %get-tuple-element.5.stored_ref, bf16[5,88,1024]{2,1,0:T(8,128)(2,1)} %get-tuple-element.6.orth_ref, bf16[5,88,1024]{2,1,0:T(8,128)(2,1)} %weight_ref.1), custom_call_target="tpu_custom_call" | custom-call | tf_op jit(solution)/shard_map/finish/pallas_call | solution.py:485

commit v3 on v2

--- a/solution.py
+++ b/solution.py
@@ -11,9 +11,9 @@
 ITERS = 2
 ROW_TILE = 8
 KERNEL_VMEM = 56 * 1024 * 1024
-PARTS = 4
-LOOK_AHEAD = 4
-GATHER_TURNS = 3
+PARTS = 2
+LOOK_AHEAD = 6
+GATHER_TURNS = 2
 
 
 EPSILON = 1e-07
@@ -82,11 +82,12 @@
     gather_recv,
     return_send,
     return_recv,
-    out_sem,
+    stored_sem,
+    orth_sem,
 ):
     rep = lax.axis_index("replica")
     me = lax.axis_index("fsdp")
-    row_count, col_count = own.shape[1:]
+    row_count, col_count = returned.shape[1:]
     width = col_count // PARTS
     units = count * PARTS
     chips = n_fsdp // 2
@@ -102,10 +103,16 @@
     def columns(part):
         return pl.ds(pl.multiple_of(part * width, 128), width)
 
-    load_grads = pltpu.make_async_copy(grads_ref, own, load_sem.at[0])
-    load_old = pltpu.make_async_copy(momentum_ref, old, load_sem.at[1])
-    load_grads.start()
-    load_old.start()
+    loads = []
+    for part in range(PARTS):
+        cols = pl.ds(part * width, width)
+        for place, (source, held) in enumerate(((grads_ref, own), (momentum_ref, old))):
+            loads.append(
+                pltpu.make_async_copy(
+                    source.at[:, :, cols], held.at[:, part], load_sem.at[place, part]
+                )
+            )
+            loads[-1].start()
 
     barrier = pltpu.get_barrier_semaphore()
     for step in range(1, n_fsdp):
@@ -121,37 +128,34 @@
 
     inner = (rep > 0) & (rep < n_rep - 1)
     pl.semaphore_wait(barrier, jnp.where(inner, n_fsdp + 1, n_fsdp))
-    load_grads.wait()
-    load_old.wait()
+    for copy in loads:
+        copy.wait()
 
     def right_copy(group, unit, raw=False):
-        mat, cols = unit // PARTS, columns(lax.rem(unit, PARTS))
-        held = own.at[group * count + mat] if raw else from_left.at[group, mat]
+        mat, part = unit // PARTS, lax.rem(unit, PARTS)
         return pltpu.make_async_remote_copy(
-            src_ref=held.at[:, cols],
-            dst_ref=from_left.at[group, mat, :, cols],
+            src_ref=own.at[group * count + mat, part] if raw else from_left.at[group, unit],
+            dst_ref=from_left.at[group, unit],
             send_sem=right_send.at[group, unit],
             recv_sem=right_recv.at[group, unit],
             device_id={"replica": rep + 1},
         )
 
     def left_copy(group, unit, raw=False):
-        mat, cols = unit // PARTS, columns(lax.rem(unit, PARTS))
-        held = own.at[group * count + mat] if raw else from_right.at[group, mat]
+        mat, part = unit // PARTS, lax.rem(unit, PARTS)
         return pltpu.make_async_remote_copy(
-            src_ref=held.at[:, cols],
-            dst_ref=from_right.at[group, mat, :, cols],
+            src_ref=own.at[group * count + mat, part] if raw else from_right.at[group, unit],
+            dst_ref=from_right.at[group, unit],
             send_sem=left_send.at[group, unit],
             recv_sem=left_recv.at[group, unit],
             device_id={"replica": rep - 1},
         )
 
     def gather_copy(unit, job, slot, target, place):
-        mat, part = unit // PARTS, lax.rem(unit, PARTS)
-        cols = columns(part)
+        part = lax.rem(unit, PARTS)
         return pltpu.make_async_remote_copy(
-            src_ref=outgoing.at[mat, :, cols],
-            dst_ref=gathered.at[job, slot, :, cols],
+            src_ref=outgoing.at[unit],
+            dst_ref=gathered.at[job, part, slot],
             send_sem=gather_send.at[unit, place],
             recv_sem=gather_recv.at[job, slot, part],
             device_id={"fsdp": target},
@@ -166,11 +170,14 @@
             device_id={"fsdp": slot},
         )
 
-    def stored_copy(mat):
-        return pltpu.make_async_copy(stored.at[mat], stored_out.at[mat], out_sem.at[0, mat])
+    def stored_copy(unit):
+        mat, part = unit // PARTS, lax.rem(unit, PARTS)
+        return pltpu.make_async_copy(
+            stored.at[unit], stored_out.at[mat, :, columns(part)], stored_sem.at[unit]
+        )
 
     def orth_copy(mat):
-        return pltpu.make_async_copy(returned.at[mat], orth_out.at[mat], out_sem.at[1, mat])
+        return pltpu.make_async_copy(returned.at[mat], orth_out.at[mat], orth_sem.at[mat])
 
     def send_raw(unit):
         @pl.when(rep == 0)
@@ -183,26 +190,29 @@
             for group in range(n_rep - 1):
                 left_copy(group, unit, raw=True).start()
 
-    def forward(unit):
-        mat, cols = unit // PARTS, columns(lax.rem(unit, PARTS))
-        for step in range(n_rep - 1):
-            high, low = n_rep - 1 - step, step
-
-            @pl.when((rep > 0) & (rep < high))
+    def forward_right(unit):
+        mat, part = unit // PARTS, lax.rem(unit, PARTS)
+        for group in range(n_rep - 1, 1, -1):
+
+            @pl.when(rep < group)
             def _():
-                right_copy(high, unit).wait_recv()
-                from_left[high, mat, :, cols] = add_rows(
-                    from_left[high, mat, :, cols], own[high * count + mat, :, cols]
+                right_copy(group, unit).wait_recv()
+                from_left[group, unit] = add_rows(
+                    from_left[group, unit], own[group * count + mat, part]
                 ).astype(jnp.bfloat16)
-                right_copy(high, unit).start()
-
-            @pl.when((rep < n_rep - 1) & (rep > low))
+                right_copy(group, unit).start()
+
+    def forward_left(unit):
+        mat, part = unit // PARTS, lax.rem(unit, PARTS)
+        for group in range(n_rep - 2):
+
+            @pl.when(rep > group)
             def _():
-                left_copy(low, unit).wait_recv()
-                from_right[low, mat, :, cols] = add_rows(
-                    from_right[low, mat, :, cols], own[low * count + mat, :, cols]
+                left_copy(group, unit).wait_recv()
+                from_right[group, unit] = add_rows(
+                    from_right[group, unit], own[group * count + mat, part]
                 ).astype(jnp.bfloat16)
-                left_copy(low, unit).start()
+                left_copy(group, unit).start()
 
     def each_gather(unit, act):
         mat = unit // PARTS
@@ -223,41 +233,38 @@
                 act(gather_copy(unit, 1, me, partner, 0))
 
     def finish_sum(unit):
-        mat, cols = unit // PARTS, columns(lax.rem(unit, PARTS))
-        total[...] = own[rep * count + mat, :, cols].astype(jnp.float32)
+        mat, part = unit // PARTS, lax.rem(unit, PARTS)
+        total[...] = own[rep * count + mat, part].astype(jnp.float32)
 
         @pl.when(rep > 0)
         def _():
             right_copy(rep, unit).wait_recv()
-            total[...] += from_left[rep, mat, :, cols].astype(jnp.float32)
+            total[...] += from_left[rep, unit].astype(jnp.float32)
 
         @pl.when(rep < n_rep - 1)
         def _():
             left_copy(rep, unit).wait_recv()
-            total[...] += from_right[rep, mat, :, cols].astype(jnp.float32)
+            total[...] += from_right[rep, unit].astype(jnp.float32)
 
         summed = total[...]
         active = owners_ref[rep * count + mat] < n_fsdp
         decay = jnp.where(active, jnp.float32(MOMENTUM_DECAY), jnp.float32(1.0))
         gain = jnp.where(active, jnp.float32(1.0), jnp.float32(0.0))
-        kept = (decay * old[mat, :, cols].astype(jnp.float32) + gain * summed).astype(jnp.bfloat16)
-        stored[mat, :, cols] = kept
+        kept = (decay * old[mat, part].astype(jnp.float32) + gain * summed).astype(jnp.bfloat16)
+        stored[unit] = kept
+        stored_copy(unit).start()
         nesterov = (summed + MOMENTUM_DECAY * kept.astype(jnp.float32)).astype(jnp.bfloat16)
-        outgoing[mat, :, cols] = nesterov
+        outgoing[unit] = nesterov
 
         @pl.when((mat < early_count) & (me == early_owner(mat)))
         def _():
-            gathered[0, me, :, cols] = nesterov
+            gathered[0, part, me] = nesterov
 
         @pl.when((mat >= early_count) & (core == mat - early_count))
         def _():
-            gathered[1, me, :, cols] = nesterov
+            gathered[1, part, me] = nesterov
 
         each_gather(unit, lambda copy: copy.start())
-
-        @pl.when(lax.rem(unit, PARTS) == PARTS - 1)
-        def _():
-            stored_copy(mat).start()
 
     def make_gram():
         held = iterate[...]
@@ -285,9 +292,10 @@
         scaled = gathered[job].astype(jnp.float32)
         frobenius = jnp.sqrt(jnp.sum(scaled * scaled))
         inverse = 1.0 / (frobenius + EPSILON)
-        iterate[...] = (
-            (scaled * inverse).reshape(n_fsdp * row_count, col_count).astype(jnp.bfloat16)
-        )
+        for part in range(PARTS):
+            iterate[:, pl.ds(part * width, width)] = (
+                (scaled[part] * inverse).reshape(n_fsdp * row_count, width).astype(jnp.bfloat16)
+            )
         whole = pl.ds(0, n_fsdp * row_count)
         for turn in range(ITERS - 1):
             make_gram()
@@ -317,20 +325,35 @@
             return_copy(1, mat, partner).start()
             returned[mat] = finished[1, me]
 
-    ahead = LOOK_AHEAD
+    ahead = min(LOOK_AHEAD, units)
     for unit in range(ahead):
         send_raw(unit)
 
-    @pl.loop(0, units)
+    right_lag, left_lag = rep - 1, n_rep - 2 - rep
+    sum_lag = jnp.maximum(right_lag, left_lag)
+
+    @pl.loop(0, units + n_rep - 2)
     def _(turn):
         @pl.when(turn < units - ahead)
         def _():
             send_raw(turn + ahead)
 
-        forward(turn)
-        finish_sum(turn)
-        last = turn == units - 1
-        early = has_early & (turn == (chip + 1) * PARTS - 1 + GATHER_TURNS)
+        to_right, to_left, to_sum = turn - right_lag, turn - left_lag, turn - sum_lag
+
+        @pl.when((rep > 0) & (to_right >= 0) & (to_right < units))
+        def _():
+            forward_right(to_right)
+
+        @pl.when((rep < n_rep - 1) & (to_left >= 0) & (to_left < units))
+        def _():
+            forward_left(to_left)
+
+        @pl.when((to_sum >= 0) & (to_sum < units))
+        def _():
+            finish_sum(to_sum)
+
+        last = to_sum == units - 1
+        early = has_early & (to_sum == (chip + 1) * PARTS - 1 + GATHER_TURNS)
 
         @pl.when(last | early)
         def _():
@@ -362,10 +385,10 @@
                 left_copy(group, unit).wait_send()
 
         each_gather(unit, lambda copy: copy.wait_send())
+        stored_copy(unit).wait()
 
     @pl.loop(0, count)
     def _(mat):
-        stored_copy(mat).wait()
         orth_copy(mat).wait()
 
     @pl.when(has_early)
@@ -382,6 +405,7 @@
     all_rows = n_fsdp * row_count
     units = count * PARTS
     block = (row_count, col_count)
+    piece = (row_count, col_count // PARTS)
     half = jnp.bfloat16
     shape = jax.ShapeDtypeStruct(momentum.shape, half)
     dma = pltpu.SemaphoreType.DMA
@@ -395,20 +419,20 @@
         ],
         out_specs=(pl.BlockSpec(memory_space=pl.ANY), pl.BlockSpec(memory_space=pl.ANY)),
         scratch_shapes=[
-            pltpu.VMEM((n_rep * count, *block), half),
-            pltpu.VMEM((count, *block), half),
-            pltpu.VMEM((n_rep, count, *block), half),
-            pltpu.VMEM((n_rep, count, *block), half),
-            pltpu.VMEM((row_count, col_count // PARTS), jnp.float32),
-            pltpu.VMEM((count, *block), half),
-            pltpu.VMEM((count, *block), half),
-            pltpu.VMEM((2, n_fsdp, *block), half),
+            pltpu.VMEM((n_rep * count, PARTS, *piece), half),
+            pltpu.VMEM((count, PARTS, *piece), half),
+            pltpu.VMEM((n_rep, units, *piece), half),
+            pltpu.VMEM((n_rep, units, *piece), half),
+            pltpu.VMEM(piece, jnp.float32),
+            pltpu.VMEM((units, *piece), half),
+            pltpu.VMEM((units, *piece), half),
+            pltpu.VMEM((2, PARTS, n_fsdp, *piece), half),
             pltpu.VMEM((all_rows, col_count), half),
             pltpu.VMEM((all_rows, all_rows), half),
             pltpu.VMEM((all_rows, all_rows), half),
             pltpu.VMEM((2, n_fsdp, *block), half),
             pltpu.VMEM((count, *block), half),
-            dma((2,)),
+            dma((2, PARTS)),
             dma((n_rep, units)),
             dma((n_rep, units)),
             dma((n_rep, units)),
@@ -417,7 +441,8 @@
             dma((2, n_fsdp, PARTS)),
             dma((2, n_fsdp)),
             dma((count,)),
-            dma((2, count)),
+            dma((units,)),
+            dma((count,)),
         ],
         compiler_params=pltpu.CompilerParams(
             collective_id=0, has_side_effects=True, vmem_limit_bytes=KERNEL_VMEM

time: 171 us -> 98.9 us (0.58)
  the two profiles are of different devices: /device:TPU:1 before, /device:TPU:2 now
where the time goes in v3:
time: 98.9 us; the launch traced here: 98.7 us
  Pallas kernels  98.1 us (99%)
    pallas_call x1, Pallas kernels, fused_sum_and_orthogonalize(): pl.pallas_call(functools.partial(fused_kernel, n_rep, n_fsdp, count), out...  94.5 us
    pallas_call x1, Pallas kernels, finish(): pl.pallas_call(functools.partial(finish_kernel, n_fsdp, update_scale), ou...  3.55 us

profile of v3, /device:TPU:2, one launch (start us, length us, event | category | flops | bytes accessed | tf_op | source)
XLA Modules:
  0.0 98.7 jit_solution(3367311246614383377)
XLA Ops:
  0.6 94.5 %sum_and_orthogonalize.1 = (bf16[5,88,1024]{2,1,0:T(8,128)(2,1)}, bf16[5,88,1024]{2,1,0:T(8,128)(2,1)}) custom-call(s32[20]{0:T(128)} %owners_ref.3, bf16[20,88,1024]{2,1,0:T(8,128)(2,1)} %bitcast.1, bf16[5,88,1024]{2,1,0:T(8,128)(2,1)} %momentum_ref.1), custom_call_target="tpu_custom_call" | custom-call | tf_op jit(solution)/shard_map/sum_and_orthogonalize/pallas_call | solution.py:412
  95.2 3.6 %finish.1 = (bf16[5,88,1024]{2,1,0:T(8,128)(2,1)}, bf16[5,88,1024]{2,1,0:T(8,128)(2,1)}, bf16[5,88,1024]{2,1,0:T(8,128)(2,1)}) custom-call(s32[20]{0:T(128)} %owners_ref.3, bf16[5,88,1024]{2,1,0:T(8,128)(2,1)} %get-tuple-element.5.stored_ref, bf16[5,88,1024]{2,1,0:T(8,128)(2,1)} %get-tuple-element.6.orth_ref, bf16[5,88,1024]{2,1,0:T(8,128)(2,1)} %weight_ref.1), custom_call_target="tpu_custom_call" | custom-call | tf_op jit(solution)/shard_map/finish/pallas_call | solution.py:510

commit v4 on v3

--- a/solution.py
+++ b/solution.py
@@ -91,14 +91,8 @@
     width = col_count // PARTS
     units = count * PARTS
     chips = n_fsdp // 2
-    early_count = count - 2
     chip, core = me // 2, lax.rem(me, 2)
     partner = me + 1 - 2 * core
-
-    has_early = (core == 1) & (chip < early_count)
-
-    def early_owner(mat):
-        return mat * 2 + 1
 
     def columns(part):
         return pl.ds(pl.multiple_of(part * width, 128), width)
@@ -151,23 +145,23 @@
             device_id={"replica": rep - 1},
         )
 
-    def gather_copy(unit, job, slot, target, place):
-        part = lax.rem(unit, PARTS)
+    def gather_copy(unit, slot, target, place):
+        mat, part = unit // PARTS, lax.rem(unit, PARTS)
         return pltpu.make_async_remote_copy(
             src_ref=outgoing.at[unit],
-            dst_ref=gathered.at[job, part, slot],
+            dst_ref=gathered.at[mat // 2, part, slot],
             send_sem=gather_send.at[unit, place],
-            recv_sem=gather_recv.at[job, slot, part],
+            recv_sem=gather_recv.at[mat // 2, slot, part],
             device_id={"fsdp": target},
         )
 
-    def return_copy(job, mat, slot):
+    def return_copy(mat):
         return pltpu.make_async_remote_copy(
-            src_ref=finished.at[job, slot],
+            src_ref=finished.at[mat // 2],
             dst_ref=returned.at[mat],
-            send_sem=return_send.at[job, slot],
+            send_sem=return_send.at[mat // 2],
             recv_sem=return_recv.at[mat],
-            device_id={"fsdp": slot},
+            device_id={"fsdp": partner},
         )
 
     def stored_copy(unit):
@@ -215,22 +209,13 @@
                 left_copy(group, unit).start()
 
     def each_gather(unit, act):
-        mat = unit // PARTS
-        late_core = mat - early_count
-
-        @pl.when((mat < early_count) & (me != early_owner(mat)))
-        def _():
-            act(gather_copy(unit, 0, me, early_owner(mat), 0))
-
-        @pl.when(mat >= early_count)
-        def _():
-            for step in range(1, chips):
-                target = lax.rem(chip + step, chips) * 2 + late_core
-                act(gather_copy(unit, 1, me, target, step))
-
-            @pl.when(core != late_core)
-            def _():
-                act(gather_copy(unit, 1, me, partner, 0))
+        solver = lax.rem(unit // PARTS, 2)
+        for step in range(1, chips):
+            act(gather_copy(unit, me, lax.rem(chip + step, chips) * 2 + solver, step))
+
+        @pl.when(core != solver)
+        def _():
+            act(gather_copy(unit, me, partner, 0))
 
     def finish_sum(unit):
         mat, part = unit // PARTS, lax.rem(unit, PARTS)
@@ -256,13 +241,9 @@
         nesterov = (summed + MOMENTUM_DECAY * kept.astype(jnp.float32)).astype(jnp.bfloat16)
         outgoing[unit] = nesterov
 
-        @pl.when((mat < early_count) & (me == early_owner(mat)))
-        def _():
-            gathered[0, part, me] = nesterov
-
-        @pl.when((mat >= early_count) & (core == mat - early_count))
-        def _():
-            gathered[1, part, me] = nesterov
+        @pl.when(core == lax.rem(mat, 2))
+        def _():
+            gathered[mat // 2, part, me] = nesterov
 
         each_gather(unit, lambda copy: copy.start())
 
@@ -282,48 +263,40 @@
         product = jnp.dot(poly[rows, :], iterate[...], preferred_element_type=jnp.float32)
         return COEFF_LINEAR * iterate[rows, :].astype(jnp.float32) + product
 
-    def orthogonalize(job, mat):
+    whole = pl.ds(0, n_fsdp * row_count)
+
+    def normalize(mat):
         @pl.loop(1, n_fsdp)
         def _(step):
             for part in range(PARTS):
-                unit = mat * PARTS + part
-                gather_copy(unit, job, lax.rem(me + step, n_fsdp), me, 0).wait_recv()
-
-        scaled = gathered[job].astype(jnp.float32)
+                gather_copy(mat * PARTS + part, lax.rem(me + step, n_fsdp), me, 0).wait_recv()
+
+        scaled = gathered[mat // 2].astype(jnp.float32)
         frobenius = jnp.sqrt(jnp.sum(scaled * scaled))
         inverse = 1.0 / (frobenius + EPSILON)
         for part in range(PARTS):
             iterate[:, pl.ds(part * width, width)] = (
                 (scaled[part] * inverse).reshape(n_fsdp * row_count, width).astype(jnp.bfloat16)
             )
-        whole = pl.ds(0, n_fsdp * row_count)
-        for turn in range(ITERS - 1):
-            make_gram()
-            make_poly(whole)
-            iterate[...] = apply_poly(whole).astype(jnp.bfloat16)
         make_gram()
 
-        @pl.when(job == 0)
-        def _():
-            make_poly(whole)
-            finished[0] = (
-                apply_poly(whole).reshape(n_fsdp, row_count, col_count).astype(jnp.bfloat16)
-            )
-
-            @pl.loop(1, n_fsdp)
-            def _(step):
-                return_copy(0, mat, lax.rem(me + step, n_fsdp)).start()
-
-            returned[mat] = finished[0, me]
-
-        @pl.when(job == 1)
-        def _():
-            pair = pl.ds(pl.multiple_of(chip * (2 * row_count), 16), 2 * row_count)
-            make_poly(pair)
-            rows = apply_poly(pair).reshape(2, row_count, col_count).astype(jnp.bfloat16)
-            finished[1, pl.ds(chip * 2, 2)] = rows
-            return_copy(1, mat, partner).start()
-            returned[mat] = finished[1, me]
+    def iterate_once():
+        make_poly(whole)
+        iterate[...] = apply_poly(whole).astype(jnp.bfloat16)
+
+    def last_iterate(mat):
+        make_gram()
+        pair = pl.ds(pl.multiple_of(chip * (2 * row_count), 16), 2 * row_count)
+        make_poly(pair)
+        rows = apply_poly(pair).reshape(2, row_count, col_count).astype(jnp.bfloat16)
+        for side in range(2):
+
+            @pl.when(core == side)
+            def _():
+                returned[mat] = rows[side]
+                finished[mat // 2] = rows[1 - side]
+
+        return_copy(mat).start()
 
     ahead = min(LOOK_AHEAD, units)
     for unit in range(ahead):
@@ -332,7 +305,7 @@
     right_lag, left_lag = rep - 1, n_rep - 2 - rep
     sum_lag = jnp.maximum(right_lag, left_lag)
 
-    @pl.loop(0, units + n_rep - 2)
+    @pl.loop(0, units + GATHER_TURNS + 2 + n_rep - 2)
     def _(turn):
         @pl.when(turn < units - ahead)
         def _():
@@ -352,23 +325,28 @@
         def _():
             finish_sum(to_sum)
 
-        last = to_sum == units - 1
-        early = has_early & (to_sum == (chip + 1) * PARTS - 1 + GATHER_TURNS)
-
-        @pl.when(last | early)
-        def _():
-            job = jnp.where(last, 1, 0)
-            orthogonalize(job, jnp.where(last, early_count + core, chip))
+        place = to_sum - GATHER_TURNS - (core + 1) * PARTS + 1
+        mat = place // (2 * PARTS) * 2 + core
+        stage = lax.rem(place, 2 * PARTS)
+        ready = (place >= 0) & (mat < count)
+
+        @pl.when(ready & (stage == 0))
+        def _():
+            normalize(mat)
+
+        @pl.when(ready & (stage == 1))
+        def _():
+            iterate_once()
+
+        @pl.when(ready & (stage == 2))
+        def _():
+            last_iterate(mat)
 
     @pl.loop(0, count)
     def _(mat):
-        held_here = jnp.where(
-            mat < early_count, me == early_owner(mat), core == mat - early_count
-        )
-
-        @pl.when(jnp.logical_not(held_here))
-        def _():
-            return_copy(0, mat, me).wait_recv()
+        @pl.when(core != lax.rem(mat, 2))
+        def _():
+            return_copy(mat).wait_recv()
 
         orth_copy(mat).start()
 
@@ -391,19 +369,18 @@
     def _(mat):
         orth_copy(mat).wait()
 
-    @pl.when(has_early)
-    def _():
-        @pl.loop(1, n_fsdp)
-        def _(step):
-            return_copy(0, chip, lax.rem(me + step, n_fsdp)).wait_send()
-
-    return_copy(1, early_count + core, partner).wait_send()
+    @pl.loop(0, count)
+    def _(mat):
+        @pl.when(core == lax.rem(mat, 2))
+        def _():
+            return_copy(mat).wait_send()
 
 
 def fused_sum_and_orthogonalize(n_rep, n_fsdp, owners, grads, momentum):
     count, row_count, col_count = momentum.shape
     all_rows = n_fsdp * row_count
     units = count * PARTS
+    jobs = (count + 1) // 2
     block = (row_count, col_count)
     piece = (row_count, col_count // PARTS)
     half = jnp.bfloat16
@@ -426,11 +403,11 @@
             pltpu.VMEM(piece, jnp.float32),
             pltpu.VMEM((units, *piece), half),
             pltpu.VMEM((units, *piece), half),
-            pltpu.VMEM((2, PARTS, n_fsdp, *piece), half),
+            pltpu.VMEM((jobs, PARTS, n_fsdp, *piece), half),
             pltpu.VMEM((all_rows, col_count), half),
             pltpu.VMEM((all_rows, all_rows), half),
             pltpu.VMEM((all_rows, all_rows), half),
-            pltpu.VMEM((2, n_fsdp, *block), half),
+            pltpu.VMEM((jobs, *block), half),
             pltpu.VMEM((count, *block), half),
             dma((2, PARTS)),
             dma((n_rep, units)),
@@ -438,8 +415,8 @@
             dma((n_rep, units)),
             dma((n_rep, units)),
             dma((units, n_fsdp // 2)),
-            dma((2, n_fsdp, PARTS)),
-            dma((2, n_fsdp)),
+            dma((jobs, n_fsdp, PARTS)),
+            dma((jobs,)),
             dma((count,)),
             dma((units,)),
             dma((count,)),
@@ -553,10 +530,10 @@
     update_scale = UPDATE_RATIO * math.sqrt(max(row_count * n_fsdp, col_count))
     offset = lax.axis_index("replica") * count
     active = lax.dynamic_slice_in_dim(owners, offset, count) < n_fsdp
-    held_bytes = 2 * row_count * col_count * (3 * n_rep * count + 4 * count + 8 * n_fsdp)
+    held_bytes = 2 * row_count * col_count * (3 * n_rep * count + 5 * count + (count + 5) * n_fsdp // 2)
     fits = held_bytes < KERNEL_VMEM // 2 and row_count % ROW_TILE == 0
     fits = fits and col_count % (128 * PARTS) == 0
-    if not fits or n_fsdp % 2 or n_rep < 2 or not 3 <= count <= n_fsdp // 2 + 2:
+    if not fits or n_fsdp % 2 or n_rep < 2:
         return by_collectives(grads, momentum, weight, active, update_scale)
     stored, orth = fused_sum_and_orthogonalize(n_rep, n_fsdp, owners, grads[0], momentum)
     return finish(n_fsdp, update_scale, owners, stored, orth, weight)

time: 98.9 us -> 91.7 us (0.927)
  the two profiles are of different devices: /device:TPU:2 before, /device:TPU:1 now
where the time goes in v4:
time: 91.7 us; the launch traced here: 91.5 us
  Pallas kernels  90.9 us (99%)
    pallas_call x1, Pallas kernels, fused_sum_and_orthogonalize(): pl.pallas_call(functools.partial(fused_kernel, n_rep, n_fsdp, count), out...  87.3 us
    pallas_call x1, Pallas kernels, finish(): pl.pallas_call(functools.partial(finish_kernel, n_fsdp, update_scale), ou...  3.55 us

profile of v4, /device:TPU:1, one launch (start us, length us, event | category | flops | bytes accessed | tf_op | source)
XLA Modules:
  0.0 91.5 jit_solution(15288427990837312489)
XLA Ops:
  0.6 87.3 %sum_and_orthogonalize.1 = (bf16[5,88,1024]{2,1,0:T(8,128)(2,1)}, bf16[5,88,1024]{2,1,0:T(8,128)(2,1)}) custom-call(s32[20]{0:T(128)} %owners_ref.3, bf16[20,88,1024]{2,1,0:T(8,128)(2,1)} %bitcast.1, bf16[5,88,1024]{2,1,0:T(8,128)(2,1)} %momentum_ref.1), custom_call_target="tpu_custom_call" | custom-call | tf_op jit(solution)/shard_map/sum_and_orthogonalize/pallas_call | solution.py:389
  87.9 3.6 %finish.1 = (bf16[5,88,1024]{2,1,0:T(8,128)(2,1)}, bf16[5,88,1024]{2,1,0:T(8,128)(2,1)}, bf16[5,88,1024]{2,1,0:T(8,128)(2,1)}) custom-call(s32[20]{0:T(128)} %owners_ref.3, bf16[5,88,1024]{2,1,0:T(8,128)(2,1)} %get-tuple-element.5.stored_ref, bf16[5,88,1024]{2,1,0:T(8,128)(2,1)} %get-tuple-element.6.orth_ref, bf16[5,88,1024]{2,1,0:T(8,128)(2,1)} %weight_ref.1), custom_call_target="tpu_custom_call" | custom-call | tf_op jit(solution)/shard_map/finish/pallas_call | solution.py:487

commit v5 on v4

--- a/solution.py
+++ b/solution.py
@@ -12,6 +12,7 @@
 ROW_TILE = 8
 KERNEL_VMEM = 56 * 1024 * 1024
 PARTS = 2
+GRAM_TILE = 256
 LOOK_AHEAD = 6
 GATHER_TURNS = 2
 
@@ -98,9 +99,9 @@
         return pl.ds(pl.multiple_of(part * width, 128), width)
 
     loads = []
-    for part in range(PARTS):
-        cols = pl.ds(part * width, width)
-        for place, (source, held) in enumerate(((grads_ref, own), (momentum_ref, old))):
+    for place, (source, held) in enumerate(((grads_ref, own), (momentum_ref, old))):
+        for part in range(PARTS):
+            cols = pl.ds(part * width, width)
             loads.append(
                 pltpu.make_async_copy(
                     source.at[:, :, cols], held.at[:, part], load_sem.at[place, part]
@@ -122,8 +123,7 @@
 
     inner = (rep > 0) & (rep < n_rep - 1)
     pl.semaphore_wait(barrier, jnp.where(inner, n_fsdp + 1, n_fsdp))
-    for copy in loads:
-        copy.wait()
+    loads[0].wait()
 
     def right_copy(group, unit, raw=False):
         mat, part = unit // PARTS, lax.rem(unit, PARTS)
@@ -248,10 +248,18 @@
         each_gather(unit, lambda copy: copy.start())
 
     def make_gram():
-        held = iterate[...]
-        gram[...] = lax.dot_general(
-            held, held, (((1,), (1,)), ((), ())), preferred_element_type=jnp.float32
-        ).astype(jnp.bfloat16)
+        rows = n_fsdp * row_count
+        for low in range(0, rows, GRAM_TILE):
+            high = min(low + GRAM_TILE, rows)
+            block = lax.dot_general(
+                iterate[low:, :],
+                iterate[low:high, :],
+                (((1,), (1,)), ((), ())),
+                preferred_element_type=jnp.float32,
+            )
+            gram[low:, low:high] = block.astype(jnp.bfloat16)
+            if high < rows:
+                gram[low:high, high:] = block[high - low :, :].T.astype(jnp.bfloat16)
 
     def make_poly(rows):
         square = jnp.dot(gram[rows, :], gram[...], preferred_element_type=jnp.float32)
@@ -299,7 +307,10 @@
         return_copy(mat).start()
 
     ahead = min(LOOK_AHEAD, units)
-    for unit in range(ahead):
+    send_raw(0)
+    for copy in loads[1:]:
+        copy.wait()
+    for unit in range(1, ahead):
         send_raw(unit)
 
     right_lag, left_lag = rep - 1, n_rep - 2 - rep

time: 91.7 us -> 89.6 us (0.977)
  Pallas kernels: 90.9 us -> 88.8 us
    pallas_call x1, Pallas kernels: 87.3 us -> 85.2 us  [fused_sum_and_orthogonalize(): pl.pallas_call(functools.partial(fused_kernel, n_rep, n_fsdp, count), out...]
where the time goes in v5:
time: 89.6 us; the launch traced here: 89.4 us
  Pallas kernels  88.8 us (99%)
    pallas_call x1, Pallas kernels, fused_sum_and_orthogonalize(): pl.pallas_call(functools.partial(fused_kernel, n_rep, n_fsdp, count), out...  85.2 us
    pallas_call x1, Pallas kernels, finish(): pl.pallas_call(functools.partial(finish_kernel, n_fsdp, update_scale), ou...  3.55 us

profile of v5, /device:TPU:1, one launch (start us, length us, event | category | flops | bytes accessed | tf_op | source)
XLA Modules:
  0.0 89.4 jit_solution(1665716925879249327)
XLA Ops:
  0.6 85.2 %sum_and_orthogonalize.1 = (bf16[5,88,1024]{2,1,0:T(8,128)(2,1)}, bf16[5,88,1024]{2,1,0:T(8,128)(2,1)}) custom-call(s32[20]{0:T(128)} %owners_ref.3, bf16[20,88,1024]{2,1,0:T(8,128)(2,1)} %bitcast.1, bf16[5,88,1024]{2,1,0:T(8,128)(2,1)} %momentum_ref.1), custom_call_target="tpu_custom_call" | custom-call | tf_op jit(solution)/shard_map/sum_and_orthogonalize/pallas_call | solution.py:400
  85.9 3.6 %finish.1 = (bf16[5,88,1024]{2,1,0:T(8,128)(2,1)}, bf16[5,88,1024]{2,1,0:T(8,128)(2,1)}, bf16[5,88,1024]{2,1,0:T(8,128)(2,1)}) custom-call(s32[20]{0:T(128)} %owners_ref.3, bf16[5,88,1024]{2,1,0:T(8,128)(2,1)} %get-tuple-element.5.stored_ref, bf16[5,88,1024]{2,1,0:T(8,128)(2,1)} %get-tuple-element.6.orth_ref, bf16[5,88,1024]{2,1,0:T(8,128)(2,1)} %weight_ref.1), custom_call_target="tpu_custom_call" | custom-call | tf_op jit(solution)/shard_map/finish/pallas_call | solution.py:498
